TPU v7x, 32 devices: a whole 2x2x4 slice. The times are simulated.
32 devices in a mesh: frame: 8 (over y, x, core), row: 4 (over z).
Axes of the slice: x: 2, y: 2, z: 4, core: 2. Of those that a mesh axis runs over, the one named last changes fastest.
Arguments:
- query_tok: bfloat16 [8, 32, 16, 2560], P('frame', 'row'), may hold values from -6 to 6
- key_tok: bfloat16 [8, 32, 16, 2560], P('frame', 'row'), may hold values from -6 to 6
- value_tok: bfloat16 [8, 32, 16, 2560], P('frame', 'row'), may hold values from -6 to 6
- grad_out: bfloat16 [8, 32, 16, 2560], P('frame', 'row'), may hold values from -6 to 6
- head_reach: int32 [20], replicated, may hold values from 0 to 1
- tile_offset: int32 [8, 8], P(None, 'row'), may hold values from -1 to 0
Outputs:
- grad_query: bfloat16 [8, 32, 16, 2560], P('frame', 'row')
- grad_key: bfloat16 [8, 32, 16, 2560], P('frame', 'row')
- grad_value: bfloat16 [8, 32, 16, 2560], P('frame', 'row')
All inputs are finite; a program needn't handle non-finite values.
Results may differ from a plain program's by a relative error of at most 0.011.
Values may be sent and summed in bfloat16 or wider, within the bound.
A program may use at most 64 MiB of HBM per device.

v0:
```python
import math

import jax
import jax.numpy as jnp
from jax import lax
from jax.sharding import PartitionSpec as P


def from_behind(block, axis, distance):
    devices = range(lax.axis_size(axis))
    route = [(i - distance, i) for i in devices if i - distance in devices]
    return lax.ppermute(block, axis, route)


def extended_2(block, sides, width):
    for axis, dim in sides:
        count = lax.axis_size(axis)
        forward = [(i, i + 1) for i in range(count - 1)]
        backward = [(target, source) for source, target in forward]
        low = lax.ppermute(
            lax.slice_in_dim(block, block.shape[dim] - width, None, axis=dim), axis, forward
        )
        high = lax.ppermute(lax.slice_in_dim(block, 0, width, axis=dim), axis, backward)
        block = jnp.concatenate([low, block, high], axis=dim)
    return block


def make_windows(extended, frames):
    rows_dev = extended.shape[1] - 2
    tiles = rows_dev // 4
    width = extended.shape[2]
    trailing = extended.shape[3:]
    tail = [(0, 0)] * len(trailing)
    padded = jnp.pad(extended, [(0, 0), (0, 2), (0, 0)] + tail)
    upper_part = padded[:, 0:rows_dev].reshape((frames + 2, tiles, 4, width) + trailing)
    lower_part = padded[:, 4 : rows_dev + 4].reshape((frames + 2, tiles, 4, width) + trailing)[
        :, :, 0:2
    ]
    six_rows = jnp.concatenate([upper_part, lower_part], axis=2)
    stacked = jnp.stack([six_rows[step : step + frames] for step in range(3)], axis=2)
    return stacked.reshape((frames * tiles, 18 * width) + trailing)


def fold_terms(term, frames, rows_dev, width):
    tiles = rows_dev // 4
    trailing = term.shape[2:]
    tail = [(0, 0)] * len(trailing)
    grid = term.reshape((frames, tiles, 3, 6, width) + trailing)
    total = None
    for step in range(3):
        part = grid[:, :, step]
        first = part[:, :, 0:4].reshape((frames, rows_dev, width) + trailing)
        second = jnp.pad(part[:, :, 4:6], [(0, 0), (0, 0), (0, 2), (0, 0)] + tail).reshape(
            (frames, rows_dev, width) + trailing
        )
        rows_sum = (
            jnp.pad(first, [(0, 0), (0, 2), (0, 0)] + tail)
            + jnp.pad(second, [(0, 0), (4, 0), (0, 0)] + tail)[:, 0 : rows_dev + 2]
        )
        placed = jnp.pad(rows_sum, [(step, 2 - step)] + [(0, 0)] * (rows_sum.ndim - 1))
        total = placed if total is None else total + placed
    return total


def window_allowed(
    first_frame, frames, offsets, reach_on, row_dev, rows_dev, row_count, frame_count, width
):
    tiles = rows_dev // 4
    slots = reach_on.shape[0]
    tile_ids = jnp.arange(tiles)[:, None]
    win_rows = jnp.arange(6)[None, :]
    global_row = row_dev * rows_dev + 4 * tile_ids + win_rows - 1
    offset3 = offsets[:, :, None]
    rows_ok = (global_row >= 0) & (global_row < row_count)
    rows_ok = (
        rows_ok[None] & ((win_rows != 0) | (offset3 == -1)) & ((win_rows != 5) | (offset3 == 0))
    )
    frame_ids = first_frame + jnp.arange(frames)[:, None] + jnp.arange(3)[None, :] - 1
    frames_ok = (frame_ids >= 0) & (frame_ids < frame_count)
    heads_ok = reach_on[:, None] | (jnp.arange(3)[None, :] == 1)
    allow = (
        frames_ok[:, None, None, :, None]
        & heads_ok[None, None, :, :, None]
        & rows_ok[:, :, None, None, :]
    )
    allow = jnp.broadcast_to(allow[..., None], (frames, tiles, slots, 3, 6, width))
    return allow.reshape(frames * tiles, slots, 1, 18 * width)


def tile_attend(query_t, grad_t, key_w, value_w, allowed):
    head_dim = query_t.shape[3]
    inv_root = 1.0 / math.sqrt(head_dim)
    scores = (
        jnp.einsum("bqmd,bkmd->bmqk", query_t, key_w, preferred_element_type=jnp.float32) * inv_root
    )
    scores = jnp.where(allowed, scores, -1e30)
    top = jnp.max(scores, axis=-1, keepdims=True)
    expo = jnp.exp(scores - top)
    probs = expo / jnp.sum(expo, axis=-1, keepdims=True)
    weights = probs.astype(jnp.bfloat16)
    attended = jnp.einsum("bmqk,bkmd->bqmd", weights, value_w, preferred_element_type=jnp.float32)
    delta = jnp.transpose(jnp.sum(grad_t.astype(jnp.float32) * attended, axis=-1), (0, 2, 1))
    dprobs = jnp.einsum("bqmd,bkmd->bmqk", grad_t, value_w, preferred_element_type=jnp.float32)
    dscores = (probs * (dprobs - delta[..., None]) * inv_root).astype(jnp.bfloat16)
    grad_query = jnp.einsum(
        "bmqk,bkmd->bqmd", dscores, key_w, preferred_element_type=jnp.float32
    ).astype(jnp.bfloat16)
    key_term = jnp.einsum("bmqk,bqmd->bkmd", dscores, query_t, preferred_element_type=jnp.float32)
    value_term = jnp.einsum("bmqk,bqmd->bkmd", weights, grad_t, preferred_element_type=jnp.float32)
    return (grad_query, key_term, value_term)


def return_rims(whole):
    rows_dev = whole.shape[1] - 2
    rim_low = whole[:, 0].astype(jnp.bfloat16)
    rim_high = whole[:, rows_dev + 1].astype(jnp.bfloat16)
    from_above = from_behind(rim_low, "row", -1)
    from_below = from_behind(rim_high, "row", 1)
    own_rows = whole[:, 1 : rows_dev + 1]
    first_row = own_rows[:, 0] + from_below.astype(jnp.float32)
    last_row = own_rows[:, rows_dev - 1] + from_above.astype(jnp.float32)
    joined = jnp.concatenate(
        [first_row[:, None], own_rows[:, 1 : rows_dev - 1], last_row[:, None]], axis=1
    )
    return joined.astype(jnp.bfloat16)


def on_device(query_tok, key_tok, value_tok, grad_out, head_reach, tile_offset):
    rows_dev, width, packed = (query_tok.shape[1], query_tok.shape[2], query_tok.shape[3])
    heads = head_reach.shape[0]
    head_dim = packed // heads
    tiles = rows_dev // 4
    frame_count = lax.axis_size("frame")
    row_count = lax.axis_size("row") * rows_dev
    row_dev = lax.axis_index("row")
    frame_dev = lax.axis_index("frame")
    reach_on = head_reach == 1
    query_grid = query_tok.reshape(tiles, 4 * width, heads, head_dim)
    grad_grid = grad_out.reshape(tiles, 4 * width, heads, head_dim)
    pair_grid = jnp.stack(
        [
            key_tok.reshape(1, rows_dev, width, heads, head_dim),
            value_tok.reshape(1, rows_dev, width, heads, head_dim),
        ],
        axis=3,
    )
    extended = extended_2(pair_grid, (("frame", 0), ("row", 1)), 1)
    windows = make_windows(extended, 1)
    offsets = lax.dynamic_slice_in_dim(tile_offset, frame_dev, 1, 0)
    allowed = window_allowed(
        frame_dev, 1, offsets, reach_on, row_dev, rows_dev, row_count, frame_count, width
    )
    grad_query, key_term, value_term = tile_attend(
        query_grid, grad_grid, windows[:, :, 0], windows[:, :, 1], allowed
    )
    folded = jnp.stack(
        [fold_terms(key_term, 1, rows_dev, width), fold_terms(value_term, 1, rows_dev, width)],
        axis=3,
    )
    from_next = from_behind(folded[0], "frame", -1)
    from_prev = from_behind(folded[2], "frame", 1)
    middle = folded[1] + from_next + from_prev
    pair_grad = return_rims(middle[None])
    grad_key = pair_grad[:, :, :, 0]
    grad_value = pair_grad[:, :, :, 1]
    return (
        grad_query.reshape(1, rows_dev, width, packed),
        grad_key.reshape(1, rows_dev, width, packed),
        grad_value.reshape(1, rows_dev, width, packed),
    )


def solution(mesh):
    return jax.shard_map(
        on_device,
        mesh=mesh,
        in_specs=(
            P("frame", "row", None, None),
            P("frame", "row", None, None),
            P("frame", "row", None, None),
            P("frame", "row", None, None),
            P(),
            P(None, "row"),
        ),
        out_specs=(
            P("frame", "row", None, None),
            P("frame", "row", None, None),
            P("frame", "row", None, None),
        ),
        check_vma=False,
    )
```

profile of v0, /device:TPU:11, one launch (start us, length us, event | category | flops | bytes accessed | tf_op | source)
XLA Modules:
  0.0 185.9 jit_solution(14302555466665236649)
XLA Ops:
  0.6 1.6 stack_reshape.6
  2.9 1.4 copy.66
  4.2 2.6 %collective-permute-start.1 = (bf16[1,8,16,2,20,128]{5,2,4,3,1,0:T(8,128)(2,1)}, bf16[1,8,16,2,20,128]{5,2,4,3,1,0:T(8,128)(2,1)}, u32[]{:S(2)}, u32[]{:S(2)}) collective-permute-start(bf16[1,8,16,2,20,128]{5,2,4,3,1,0:T(8,128)(2,1)} %copy.66), channel_id=1, source_target_pairs={{4,0},{8,4},{12,8},{16,12},{20,16},{24,20},{28,24},{5,1},{9,5},{13... | collective-permute-start | bytes 3932168 | tf_op jit(solution)/shard_map/ppermute | solution.py:23
  6.8 3.9 %collective-permute-start = (bf16[1,8,16,2,20,128]{5,2,4,3,1,0:T(8,128)(2,1)}, bf16[1,8,16,2,20,128]{5,2,4,3,1,0:T(8,128)(2,1)}, u32[]{:S(2)}, u32[]{:S(2)}) collective-permute-start(bf16[1,8,16,2,20,128]{5,2,4,3,1,0:T(8,128)(2,1)} %copy.66), channel_id=1, source_target_pairs={{0,4},{4,8},{8,12},{12,16},{16,20},{20,24},{24,28},{1,5},{5,9},{9,... | collective-permute-start | bytes 3932168 | tf_op jit(solution)/shard_map/ppermute | solution.py:20
  10.8 25.5 %collective-permute-done.1 = bf16[1,8,16,2,20,128]{5,2,4,3,1,0:T(8,128)(2,1)} collective-permute-done((bf16[1,8,16,2,20,128]{5,2,4,3,1,0:T(8,128)(2,1)}, bf16[1,8,16,2,20,128]{5,2,4,3,1,0:T(8,128)(2,1)}, u32[]{:S(2)}, u32[]{:S(2)}) %collective-permute-start.1) | collective-permute-done | bytes 1310752 | tf_op jit(solution)/shard_map/ppermute | solution.py:23
  36.4 1.7 copy.69
  38.1 1.7 copy.68
  42.0 2.1 %collective-permute-start.3 = (bf16[3,1,16,2,20,128]{5,2,4,3,1,0:T(8,128)(2,1)}, bf16[3,1,16,2,20,128]{5,2,4,3,1,0:T(8,128)(2,1)}, u32[]{:S(2)}, u32[]{:S(2)}) collective-permute-start(bf16[3,1,16,2,20,128]{5,2,4,3,1,0:T(8,128)(2,1)} %copy.73), channel_id=1, source_target_pairs={{1,0},{2,1},{3,2},{5,4},{6,5},{7,6},{9,8},{10,9},{11,10},{13,12},{... | collective-permute-start | bytes 1474568 | tf_op jit(solution)/shard_map/ppermute | solution.py:23
  44.0 3.4 %collective-permute-start.2 = (bf16[3,1,16,2,20,128]{5,2,4,3,1,0:T(8,128)(2,1)}, bf16[3,1,16,2,20,128]{5,2,4,3,1,0:T(8,128)(2,1)}, u32[]{:S(2)}, u32[]{:S(2)}) collective-permute-start(bf16[3,1,16,2,20,128]{5,2,4,3,1,0:T(8,128)(2,1)} %copy.70), channel_id=1, source_target_pairs={{0,1},{1,2},{2,3},{4,5},{5,6},{6,7},{8,9},{9,10},{10,11},{12,13},{... | collective-permute-start | bytes 1474568 | tf_op jit(solution)/shard_map/ppermute | solution.py:20
  48.3 2.2 %reshape.365 = bf16[2,64,20,128]{3,2,1,0:T(8,128)(2,1)} reshape(bf16[1,8,16,2560]{3,2,1,0:T(8,128)(2,1)} %param.9) | data formatting | bytes 1310720 | tf_op jit(solution)/shard_map/reshape | solution.py:139
  50.6 2.2 %reshape.364 = bf16[2,64,20,128]{3,2,1,0:T(8,128)(2,1)} reshape(bf16[1,8,16,2560]{3,2,1,0:T(8,128)(2,1)} %param.6) | data formatting | bytes 1310720 | tf_op jit(solution)/shard_map/reshape | solution.py:138
  57.3 4.9 %pad_maximum_fusion.1 = (bf16[3,8,16,2,20,128]{5,4,2,1,3,0:T(8,128)(2,1)S(1)}, bf16[3,8,16,2,20,128]{5,4,2,1,3,0:T(8,128)(2,1)S(1)}) fusion(bf16[3,1,16,2,20,128]{5,4,2,1,3,0:T(8,128)(2,1)S(1)} %copy.71, bf16[1,8,16,2,20,128]{5,4,2,1,3,0:T(8,128)(2,1)S(1)} %copy.69, bf16[1,8,16,2,20,128]{5,4,2,1,3,0:T(8,128)(2,1)S(1)} %constant_dynamic-update-slice_fusion, ...), kind=kLoop, calls=%fused_computation.22 | loop fusion | flops 49152000 | bytes 12779520 | tf_op jit(solution)/shard_map/concatenate | solution.py:24
  68.3 7.5 %fusion.67 = (f32[2,20,64]{2,1,0:T(8,128)S(1)}, f32[2,20,64,288]{3,2,1,0:T(8,128)S(1)}) fusion(f32[2,20,288,64]{2,3,1,0:T(8,128)S(1)} %fusion.25, pred[2,20,288]{2,1,0:T(8,128)(4,1)S(1)} %broadcast_in_dim.15), kind=kOutput, calls=%fused_computation.121 | output fusion | flops 4423967 | bytes 5920000 | tf_op jit(solution)/shard_map/sub | solution.py:98
  77.0 1.6 fusion.51
  80.3 1.7 fusion.11
  87.7 2.1 %fusion.15 = (f32[10,16,2,20,128]{4,1,3,0,2:T(8,128)}, f32[10,16,2,20,128]{4,1,3,0,2:T(8,128)S(1)}) fusion(f32[3,10,16,1,20,128]{5,2,4,1,0,3:T(8,128)S(1)} %add_bitcast_fusion.1, f32[3,10,16,1,20,128]{5,2,4,1,0,3:T(8,128)S(1)} %add_bitcast_fusion), kind=kLoop, calls=%fused_computation.34 | loop fusion | flops 1638400 | bytes 16384000 | tf_op jit(solution)/shard_map/squeeze | solution.py:160
  89.8 1.9 %collective-permute-start.4 = (f32[10,16,2,20,128]{4,1,3,0,2:T(8,128)}, f32[10,16,2,20,128]{4,1,3,0,2:T(8,128)S(1)}, u32[]{:S(2)}, u32[]{:S(2)}) collective-permute-start(f32[10,16,2,20,128]{4,1,3,0,2:T(8,128)} %get-tuple-element.5), channel_id=1, source_target_pairs={{4,0},{8,4},{12,8},{16,12},{20,16},{24,20},{28,24},{5,1},{9,5},{13... | collective-permute-start | bytes 9830408 | tf_op jit(solution)/shard_map/ppermute | solution.py:12
  91.7 5.5 %collective-permute-start.5 = (f32[10,16,2,20,128]{4,1,3,0,2:T(8,128)S(1)}, f32[10,16,2,20,128]{4,1,3,0,2:T(8,128)S(1)}, u32[]{:S(2)}, u32[]{:S(2)}) collective-permute-start(f32[10,16,2,20,128]{4,1,3,0,2:T(8,128)S(1)} %get-tuple-element.6), channel_id=1, source_target_pairs={{0,4},{4,8},{8,12},{12,16},{16,20},{20,24},{24,28},{1,5},{5,9},{9,... | collective-permute-start | bytes 9830408 | tf_op jit(solution)/shard_map/ppermute | solution.py:12
  97.2 68.1 %collective-permute-done.4 = f32[10,16,2,20,128]{4,1,3,0,2:T(8,128)S(1)} collective-permute-done((f32[10,16,2,20,128]{4,1,3,0,2:T(8,128)}, f32[10,16,2,20,128]{4,1,3,0,2:T(8,128)S(1)}, u32[]{:S(2)}, u32[]{:S(2)}) %collective-permute-start.4) | collective-permute-done | bytes 3276832 | tf_op jit(solution)/shard_map/ppermute | solution.py:12
  166.7 3.2 %collective-permute-start.6 = (bf16[1,16,2,20,128]{4,1,3,2,0:T(8,128)(2,1)}, bf16[1,16,2,20,128]{4,1,3,2,0:T(8,128)(2,1)}, u32[]{:S(2)}, u32[]{:S(2)}) collective-permute-start(bf16[1,16,2,20,128]{4,1,3,2,0:T(8,128)(2,1)} %get-tuple-element.20), channel_id=1, source_target_pairs={{0,1},{1,2},{2,3},{4,5},{5,6},{6,7},{8,9},{9,10},{10,11},{12,13},{... | collective-permute-start | bytes 491528 | tf_op jit(solution)/shard_map/ppermute | solution.py:12
  169.9 2.3 %fusion.47 = bf16[2,64,20,128]{3,1,2,0:T(8,128)(2,1)S(1)} fusion(bf16[2,20,64,288]{3,2,1,0:T(8,128)(2,1)} %copy-done.2, bf16[2,288,2,20,128]{4,1,3,0,2:T(8,128)(2,1)S(1)} %bitcast.156), kind=kOutput, calls=%fused_computation.82 | convolution fusion | flops 189071360 | bytes 5079040 | tf_op jit(solution)/shard_map/bmqk,bkmd->bqmd/dot_general | solution.py:105
  173.6 2.2 %reshape.366 = bf16[1,8,16,2560]{3,2,1,0:T(8,128)(2,1)} reshape(bf16[2,64,20,128]{3,2,1,0:T(8,128)(2,1)} %copy.82) | data formatting | bytes 1310720 | tf_op jit(solution)/shard_map/reshape | solution.py:167
  175.9 2.7 %collective-permute-start.7 = (bf16[1,16,2,20,128]{4,1,3,2,0:T(8,128)(2,1)S(1)}, bf16[1,16,2,20,128]{4,1,3,2,0:T(8,128)(2,1)S(1)}, u32[]{:S(2)}, u32[]{:S(2)}) collective-permute-start(bf16[1,16,2,20,128]{4,1,3,2,0:T(8,128)(2,1)S(1)} %get-tuple-element.21), channel_id=1, source_target_pairs={{1,0},{2,1},{3,2},{5,4},{6,5},{7,6},{9,8},{10,9},{11,10},{13,12},{... | collective-permute-start | bytes 491528 | tf_op jit(solution)/shard_map/ppermute | solution.py:12
  179.8 2.8 %collective-permute-done.7 = bf16[1,16,2,20,128]{4,1,3,2,0:T(8,128)(2,1)S(1)} collective-permute-done((bf16[1,16,2,20,128]{4,1,3,2,0:T(8,128)(2,1)S(1)}, bf16[1,16,2,20,128]{4,1,3,2,0:T(8,128)(2,1)S(1)}, u32[]{:S(2)}, u32[]{:S(2)}) %collective-permute-start.7) | collective-permute-done | bytes 163872 | tf_op jit(solution)/shard_map/ppermute | solution.py:12
  (94 shorter events, 29.8 us)
Async XLA Ops:
  0.6 1.7 copy-start.4
  2.3 8.4 %copy-start.6 = (s32[20]{0:T(128)S(1)}, s32[20]{0:T(128)}, u32[]{:S(2)}) copy-start(s32[20]{0:T(128)} %param.10) | copy-start | bytes 244
  4.2 32.1 %collective-permute-start.1 = (bf16[1,8,16,2,20,128]{5,2,4,3,1,0:T(8,128)(2,1)}, bf16[1,8,16,2,20,128]{5,2,4,3,1,0:T(8,128)(2,1)}, u32[]{:S(2)}, u32[]{:S(2)}) collective-permute-start(bf16[1,8,16,2,20,128]{5,2,4,3,1,0:T(8,128)(2,1)} %copy.66), channel_id=1, source_target_pairs={{4,0},{8,4},{12,8},{16,12},{20,16},{24,20},{28,24},{5,1},{9,5},{13... | collective-permute-start | bytes 3932168 | tf_op jit(solution)/shard_map/ppermute | solution.py:23
  6.8 31.3 %collective-permute-start = (bf16[1,8,16,2,20,128]{5,2,4,3,1,0:T(8,128)(2,1)}, bf16[1,8,16,2,20,128]{5,2,4,3,1,0:T(8,128)(2,1)}, u32[]{:S(2)}, u32[]{:S(2)}) collective-permute-start(bf16[1,8,16,2,20,128]{5,2,4,3,1,0:T(8,128)(2,1)} %copy.66), channel_id=1, source_target_pairs={{0,4},{4,8},{8,12},{12,16},{16,20},{20,24},{24,28},{1,5},{5,9},{9,... | collective-permute-start | bytes 3932168 | tf_op jit(solution)/shard_map/ppermute | solution.py:20
  39.8 1.3 copy-start
  39.8 7.7 %copy-start.5 = (s32[8,2]{0,1:T(2,128)S(1)}, s32[8,2]{0,1:T(2,128)}, u32[]{:S(2)}) copy-start(s32[8,2]{0,1:T(2,128)} %param.11) | copy-start | bytes 196
  42.0 11.8 %collective-permute-start.3 = (bf16[3,1,16,2,20,128]{5,2,4,3,1,0:T(8,128)(2,1)}, bf16[3,1,16,2,20,128]{5,2,4,3,1,0:T(8,128)(2,1)}, u32[]{:S(2)}, u32[]{:S(2)}) collective-permute-start(bf16[3,1,16,2,20,128]{5,2,4,3,1,0:T(8,128)(2,1)} %copy.73), channel_id=1, source_target_pairs={{1,0},{2,1},{3,2},{5,4},{6,5},{7,6},{9,8},{10,9},{11,10},{13,12},{... | collective-permute-start | bytes 1474568 | tf_op jit(solution)/shard_map/ppermute | solution.py:23
  44.0 12.1 %collective-permute-start.2 = (bf16[3,1,16,2,20,128]{5,2,4,3,1,0:T(8,128)(2,1)}, bf16[3,1,16,2,20,128]{5,2,4,3,1,0:T(8,128)(2,1)}, u32[]{:S(2)}, u32[]{:S(2)}) collective-permute-start(bf16[3,1,16,2,20,128]{5,2,4,3,1,0:T(8,128)(2,1)} %copy.70), channel_id=1, source_target_pairs={{0,1},{1,2},{2,3},{4,5},{5,6},{6,7},{8,9},{9,10},{10,11},{12,13},{... | collective-permute-start | bytes 1474568 | tf_op jit(solution)/shard_map/ppermute | solution.py:20
  65.9 1.1 copy-start.1
  68.3 7.5 %copy-start.3 = (bf16[2,64,20,128]{3,2,1,0:T(8,128)(2,1)S(1)}, bf16[2,64,20,128]{3,2,1,0:T(8,128)(2,1)}, u32[]{:S(2)}) copy-start(bf16[2,64,20,128]{3,2,1,0:T(8,128)(2,1)} %reshape.365) | copy-start | bytes 1966084
  82.0 1.3 copy-start.2
  89.8 75.5 %collective-permute-start.4 = (f32[10,16,2,20,128]{4,1,3,0,2:T(8,128)}, f32[10,16,2,20,128]{4,1,3,0,2:T(8,128)S(1)}, u32[]{:S(2)}, u32[]{:S(2)}) collective-permute-start(f32[10,16,2,20,128]{4,1,3,0,2:T(8,128)} %get-tuple-element.5), channel_id=1, source_target_pairs={{4,0},{8,4},{12,8},{16,12},{20,16},{24,20},{28,24},{5,1},{9,5},{13... | collective-permute-start | bytes 9830408 | tf_op jit(solution)/shard_map/ppermute | solution.py:12
  91.7 73.6 %collective-permute-start.5 = (f32[10,16,2,20,128]{4,1,3,0,2:T(8,128)S(1)}, f32[10,16,2,20,128]{4,1,3,0,2:T(8,128)S(1)}, u32[]{:S(2)}, u32[]{:S(2)}) collective-permute-start(f32[10,16,2,20,128]{4,1,3,0,2:T(8,128)S(1)} %get-tuple-element.6), channel_id=1, source_target_pairs={{0,4},{4,8},{8,12},{12,16},{16,20},{20,24},{24,28},{1,5},{5,9},{9,... | collective-permute-start | bytes 9830408 | tf_op jit(solution)/shard_map/ppermute | solution.py:12
  166.7 12.1 %collective-permute-start.6 = (bf16[1,16,2,20,128]{4,1,3,2,0:T(8,128)(2,1)}, bf16[1,16,2,20,128]{4,1,3,2,0:T(8,128)(2,1)}, u32[]{:S(2)}, u32[]{:S(2)}) collective-permute-start(bf16[1,16,2,20,128]{4,1,3,2,0:T(8,128)(2,1)} %get-tuple-element.20), channel_id=1, source_target_pairs={{0,1},{1,2},{2,3},{4,5},{5,6},{6,7},{8,9},{9,10},{10,11},{12,13},{... | collective-permute-start | bytes 491528 | tf_op jit(solution)/shard_map/ppermute | solution.py:12
  175.9 6.7 %collective-permute-start.7 = (bf16[1,16,2,20,128]{4,1,3,2,0:T(8,128)(2,1)S(1)}, bf16[1,16,2,20,128]{4,1,3,2,0:T(8,128)(2,1)S(1)}, u32[]{:S(2)}, u32[]{:S(2)}) collective-permute-start(bf16[1,16,2,20,128]{4,1,3,2,0:T(8,128)(2,1)S(1)} %get-tuple-element.21), channel_id=1, source_target_pairs={{1,0},{2,1},{3,2},{5,4},{6,5},{7,6},{9,8},{10,9},{11,10},{13,12},{... | collective-permute-start | bytes 491528 | tf_op jit(solution)/shard_map/ppermute | solution.py:12
where the time goes:
time: 189 us; the launch traced here: 186 us
  waiting for transfers between devices  98.6 us (52%)
  local copies, waits for them, and re-layouts  31.2 us (17%)
  starting transfers between devices  25.2 us (13%)
  other arithmetic  20.4 us (11%)
  matrix products  9.2 us (5%)
    ppermute x4, waiting for transfers between devices, from_behind(): return lax.ppermute(block, axis, route)  70.9 us
    ppermute x2, waiting for transfers between devices, extended_2(): lax.ppermute(lax.slice_in_dim(block, 0, width, axis=dim), axis, backward)  26.5 us
    ppermute x4, starting transfers between devices, from_behind(): return lax.ppermute(block, axis, route)  13.3 us
    sub x1, other arithmetic, tile_attend(): expo = jnp.exp(scores - top)  7.52 us
    ppermute x2, starting transfers between devices, extended_2(): lax.ppermute(lax.slice_in_dim(block, block.shape[dim] - width, None, axis...  7.27 us
    concatenate x1, other arithmetic, extended_2(): block = jnp.concatenate([low, block, high], axis=dim)  4.87 us
    ppermute x2, starting transfers between devices, extended_2(): lax.ppermute(lax.slice_in_dim(block, 0, width, axis=dim), axis, backward)  4.64 us
  transfers between devices with their start and end apart: 8, of which 5 were waited for; matrix products, arithmetic and copies ran while one was open for 8% of the time, Pallas kernels for 0%

commit v1 on v0

v1 whole, which is shorter than its diff:
```python
import functools
import math

import jax
import jax.numpy as jnp
from jax import lax
from jax.experimental import pallas as pl
from jax.experimental.pallas import tpu as pltpu
from jax.sharding import PartitionSpec as P

F32 = jnp.float32
BF16 = jnp.bfloat16
MASKED = -1e30
TILE_ROWS = 4
NT = (((1,), (1,)), ((), ()))
NN = (((1,), (0,)), ((), ()))
TN = (((0,), (0,)), ((), ()))
QD, ST1, ST2, DQ = range(4)


def dot(a, b, dims):
    return lax.dot_general(a, b, dims, preferred_element_type=F32)


def kernel(
    cfg,
    info,
    penalty,
    offs,
    q_ref,
    k_ref,
    v_ref,
    g_ref,
    oq_ref,
    ok_ref,
    ov_ref,
    qg,
    kv,
    kv_in,
    qd,
    bias,
    e_s,
    dp_s,
    st_mine,
    st_in,
    tot_mine,
    tot_in,
    dq_own,
    dq_out,
    dq_in,
    dk_res,
    dv_res,
    rim_out,
    rim_in,
    kv_send,
    kv_recv,
    f_send,
    f_recv,
    r_send,
    r_recv,
):
    heads, pairs, group, width, tokens, dim, frames, blocks = cfg
    slots = pairs * group
    ext = tokens + 2 * width
    tiles = tokens // (TILE_ROWS * width)
    rows_dev = tokens // width
    inv_root = 1.0 / math.sqrt(dim)
    f = lax.axis_index("frame")
    b = lax.axis_index("row")
    f_has = (f > 0, f < frames - 1)
    b_has = (b > 0, b < blocks - 1)
    f_to = (f - 1, f + 1)
    b_to = (b - 1, b + 1)

    barrier = pltpu.get_barrier_semaphore()
    for d in range(2):

        @pl.when(f_has[d])
        def _():
            pl.semaphore_signal(
                barrier, inc=1, device_id=(f_to[d], b), device_id_type=pl.DeviceIdType.MESH
            )

        @pl.when(b_has[d])
        def _():
            pl.semaphore_signal(
                barrier, inc=1, device_id=(f, b_to[d]), device_id_type=pl.DeviceIdType.MESH
            )

    pl.semaphore_wait(barrier, sum(has.astype(jnp.int32) for has in f_has + b_has))

    def frame_copy(kind, c, d):
        src, dst = {
            QD: lambda: (qd.at[c, 0], qd.at[c, 2 - d]),
            ST1: lambda: (st_mine.at[c, 1 + d], st_in.at[c, 1 - d]),
            ST2: lambda: (tot_mine.at[c], tot_in.at[c, 1 - d]),
            DQ: lambda: (dq_out.at[c, d], dq_in.at[c, 1 - d]),
        }[kind]()
        return pltpu.make_async_remote_copy(
            src_ref=src,
            dst_ref=dst,
            send_sem=f_send.at[kind, c, d],
            recv_sem=f_recv.at[kind, c, 1 - d],
            device_id=(f_to[d], b),
            device_id_type=pl.DeviceIdType.MESH,
        )

    def frame_start(kind, c):
        for d in range(2):

            @pl.when(f_has[d])
            def _():
                frame_copy(kind, c, d).start()

    def frame_arrived(kind, c):
        for d in range(2):

            @pl.when(f_has[d])
            def _():
                frame_copy(kind, c, 1 - d).wait_recv()

    def kv_copy(which, d):
        src = (k_ref, v_ref)[which]
        first = 0 if d == 0 else tokens - width
        return pltpu.make_async_remote_copy(
            src_ref=src.at[pl.ds(first, width)],
            dst_ref=kv_in.at[1 - d, which],
            send_sem=kv_send.at[which, d],
            recv_sem=kv_recv.at[which, 1 - d],
            device_id=(f, b_to[d]),
            device_id_type=pl.DeviceIdType.MESH,
        )

    def rim_copy(first, count, sem, d):
        return pltpu.make_async_remote_copy(
            src_ref=rim_out.at[d, pl.ds(first, count)],
            dst_ref=rim_in.at[1 - d, pl.ds(first, count)],
            send_sem=r_send.at[sem, d],
            recv_sem=r_recv.at[sem, 1 - d],
            device_id=(f, b_to[d]),
            device_id_type=pl.DeviceIdType.MESH,
        )

    def rim_start(first, count, sem):
        for d in range(2):

            @pl.when(b_has[d])
            def _():
                rim_copy(first, count, sem, d).start()

    for d in range(2):

        @pl.when(b_has[d])
        def _():
            for which in range(2):
                kv_copy(which, d).start()

    def lanes(head):
        return pl.ds(pl.multiple_of(head * dim, dim), dim)

    def split_queries(h, _):
        qg[h, 0] = q_ref[:, lanes(h)]
        qg[h, 1] = g_ref[:, lanes(h)]
        return 0

    lax.fori_loop(0, heads, split_queries, 0)

    def gather(c, _):
        for j in range(group):
            qd[c, 0, j] = qg[info[0, c * group + j]]
        frame_start(QD, c)
        return 0

    lax.fori_loop(0, pairs, gather, 0)

    def split_keys(h, _):
        kv[h, 0, pl.ds(width, tokens)] = k_ref[:, lanes(h)]
        kv[h, 1, pl.ds(width, tokens)] = v_ref[:, lanes(h)]
        return 0

    lax.fori_loop(0, heads, split_keys, 0)
    for d in range(2):

        @pl.when(jnp.logical_not(b_has[d]))
        def _():
            kv_in[d] = jnp.zeros(kv_in.shape[1:], BF16)
            rim_in[d] = jnp.zeros(rim_in.shape[1:], BF16)

        if pairs:

            @pl.when(jnp.logical_not(f_has[d]))
            def _():
                qd[:, 1 + d] = jnp.zeros((pairs,) + qd.shape[2:], BF16)
                dq_in[:, d] = jnp.zeros((pairs,) + dq_in.shape[2:], BF16)
                tot_in[:, d] = jnp.zeros((pairs,) + tot_in.shape[2:], F32)
                row = lax.broadcasted_iota(jnp.int32, (pairs,) + st_in.shape[2:], 1)
                st_in[:, d] = jnp.where(row % 4 == 0, MASKED, 0.0).astype(F32)

    key_row = jnp.zeros((ext, tokens), jnp.int32)
    tile = jnp.zeros((ext, tokens), jnp.int32)
    sub = lax.broadcasted_iota(jnp.int32, (ext, tokens), 0)
    lane = lax.broadcasted_iota(jnp.int32, (ext, tokens), 1)
    for r in range(1, rows_dev + 2):
        key_row = key_row + (sub >= r * width).astype(jnp.int32)
    for t in range(1, tiles):
        tile = tile + (lane >= t * TILE_ROWS * width).astype(jnp.int32)
    global_row = b * rows_dev + key_row - 1
    row_ok = (global_row >= 0) & (global_row < blocks * rows_dev)
    for j, frame in enumerate((f, jnp.maximum(f - 1, 0), jnp.minimum(f + 1, frames - 1))):
        off = jnp.zeros((ext, tokens), F32)
        for t in range(tiles):
            off = jnp.where(tile == t, offs[frame, t], off)
        rel = (key_row - 1 - TILE_ROWS * tile).astype(F32) - off
        outside = jnp.maximum(jnp.minimum(jnp.minimum(rel, TILE_ROWS - rel), 0.0), -1.0)
        bias[:, pl.ds(j * tokens, tokens)] = jnp.where(row_ok, -outside * MASKED, MASKED)

    for d in range(2):

        @pl.when(b_has[d])
        def _():
            for which in range(2):
                kv_copy(which, 1 - d).wait_recv()

    def split_rims(h, _):
        for which in range(2):
            kv[h, which, pl.ds(0, width)] = kv_in[0, which, :, lanes(h)]
            kv[h, which, pl.ds(width + tokens, width)] = kv_in[1, which, :, lanes(h)]
        return 0

    lax.fori_loop(0, heads, split_rims, 0)

    def put_key_grads(s, dk, dv):
        dk_res[s] = dk[width : width + tokens]
        dv_res[s] = dv[width : width + tokens]
        rim_out[0, s, 0] = dk[:width].astype(BF16)
        rim_out[0, s, 1] = dv[:width].astype(BF16)
        rim_out[1, s, 0] = dk[width + tokens :].astype(BF16)
        rim_out[1, s, 1] = dv[width + tokens :].astype(BF16)

    def local_heads(i, _):
        for j in range(group):
            s = slots + i * group + j
            head = info[0, s]
            kx, vx = kv[head, 0], kv[head, 1]
            q, g = qg[head, 0], qg[head, 1]
            sc = dot(kx, q, NT) * inv_root + bias[:, pl.ds(0, tokens)]
            e = jnp.exp(sc - jnp.max(sc, axis=0, keepdims=True))
            dp = dot(vx, g, NT)
            inv = 1.0 / jnp.sum(e, axis=0, keepdims=True)
            p = e * inv
            delta = jnp.sum(p * dp, axis=0, keepdims=True)
            ds = (p * (dp - delta) * inv_root).astype(BF16)
            put_key_grads(s, dot(ds, q, NN), dot(p.astype(BF16), g, NN))
            dq_own[s] = dot(ds, kx, TN)
        return 0

    local = heads // group - pairs
    if local:
        lax.fori_loop(0, local, local_heads, 0)
        rim_start(slots, heads - slots, pairs)

    def partial_sums(c):
        frame_arrived(QD, c)
        for j in range(group):
            s = c * group + j
            head = info[0, s]
            absent = [penalty[s] + jnp.where(has, 0.0, MASKED) for has in f_has]
            kx, vx = kv[head, 0], kv[head, 1]
            q = jnp.concatenate([qd[c, part, j, 0] for part in range(3)], axis=0)
            g = jnp.concatenate([qd[c, part, j, 1] for part in range(3)], axis=0)
            sc = dot(kx, q, NT) * inv_root + bias[...]
            top = jnp.max(sc, axis=0, keepdims=True)
            e = jnp.exp(sc - top)
            dp = dot(vx, g, NT)
            e_s[s] = e
            dp_s[s] = dp
            total = jnp.sum(e, axis=0, keepdims=True)
            mixed = jnp.sum(e * dp, axis=0, keepdims=True)
            for part in range(3):
                cut = slice(part * tokens, (part + 1) * tokens)
                m = top[:, cut]
                if part:
                    m = m + absent[part - 1]
                st_mine[c, part, 4 * j : 4 * j + 1] = m
                st_mine[c, part, 4 * j + 1 : 4 * j + 2] = total[:, cut]
                st_mine[c, part, 4 * j + 2 : 4 * j + 3] = mixed[:, cut]
                st_mine[c, part, 4 * j + 3 : 4 * j + 4] = total[:, cut]
        frame_start(ST1, c)

    def combine(c):
        frame_arrived(ST1, c)
        for j in range(group):
            parts = [st_mine.at[c, 0], st_in.at[c, 0], st_in.at[c, 1]]
            m, total, mixed = [
                [p[4 * j + row : 4 * j + row + 1] for p in parts] for row in range(3)
            ]
            top = jnp.maximum(jnp.maximum(m[0], m[1]), m[2])
            scale = [jnp.exp(x - top) for x in m]
            inv = 1.0 / sum(x * y for x, y in zip(scale, total))
            tot_mine[c, 4 * j : 4 * j + 1] = top
            tot_mine[c, 4 * j + 1 : 4 * j + 2] = inv
            tot_mine[c, 4 * j + 2 : 4 * j + 3] = sum(x * y for x, y in zip(scale, mixed)) * inv
            tot_mine[c, 4 * j + 3 : 4 * j + 4] = inv
        frame_start(ST2, c)

    def backward(c):
        frame_arrived(ST2, c)
        for j in range(group):
            s = c * group + j
            kx = kv[info[0, s], 0]
            q = jnp.concatenate([qd[c, part, j, 0] for part in range(3)], axis=0)
            g = jnp.concatenate([qd[c, part, j, 1] for part in range(3)], axis=0)
            whole = [tot_mine.at[c], tot_in.at[c, 0], tot_in.at[c, 1]]
            scale = jnp.concatenate(
                [
                    jnp.exp(st_mine[c, part, 4 * j : 4 * j + 1] - whole[part][4 * j : 4 * j + 1])
                    * whole[part][4 * j + 1 : 4 * j + 2]
                    for part in range(3)
                ],
                axis=1,
            )
            delta = jnp.concatenate(
                [whole[part][4 * j + 2 : 4 * j + 3] for part in range(3)], axis=1
            )
            p = e_s[s] * scale
            ds = (p * (dp_s[s] - delta) * inv_root).astype(BF16)
            put_key_grads(s, dot(ds, q, NN), dot(p.astype(BF16), g, NN))
            dq = dot(ds, kx, TN)
            dq_own[s] = dq[:tokens]
            dq_out[c, 0, j] = dq[tokens : 2 * tokens].astype(BF16)
            dq_out[c, 1, j] = dq[2 * tokens :].astype(BF16)
        frame_start(DQ, c)
        rim_start(c * group, group, c)

    def add_queries(c):
        frame_arrived(DQ, c)
        for j in range(group):
            s = c * group + j
            dq_own[s] = dq_own[s] + (dq_in[c, 0, j].astype(F32) + dq_in[c, 1, j].astype(F32))

    def step(i, _):
        for lag, stage in enumerate((partial_sums, combine, backward, add_queries)):

            @pl.when((i >= lag) & (i < pairs + lag))
            def _():
                stage(i - lag)

        return 0

    if pairs:
        lax.fori_loop(0, pairs + 3, step, 0)

    for d in range(2):

        @pl.when(b_has[d])
        def _():
            for c in range(pairs):
                rim_copy(c * group, group, c, 1 - d).wait_recv()
            if local:
                rim_copy(slots, heads - slots, pairs, 1 - d).wait_recv()

    def assemble(h, _):
        s = info[1, h]
        cols = lanes(h)
        oq_ref[:, cols] = dq_own[s].astype(BF16)
        for which, (res, out) in enumerate(((dk_res, ok_ref), (dv_res, ov_ref))):
            full = res[s]
            first = full[:width] + rim_in[0, s, which].astype(F32)
            last = full[tokens - width :] + rim_in[1, s, which].astype(F32)
            out[:, cols] = jnp.concatenate(
                [first, full[width : tokens - width], last], axis=0
            ).astype(BF16)
        return 0

    lax.fori_loop(0, heads, assemble, 0)

    for d in range(2):

        @pl.when(b_has[d])
        def _():
            for which in range(2):
                kv_copy(which, d).wait_send()
            for c in range(pairs):
                rim_copy(c * group, group, c, d).wait_send()
            if local:
                rim_copy(slots, heads - slots, pairs, d).wait_send()

        if pairs:

            @pl.when(f_has[d])
            def _():
                def sent(c, _):
                    for kind in (QD, ST1, ST2, DQ):
                        frame_copy(kind, c, d).wait_send()
                    return 0

                lax.fori_loop(0, pairs, sent, 0)


def attention(mesh, pairs, group, width, heads, info, penalty, offs, q, k, v, g):
    tokens, packed = q.shape
    dim = packed // heads
    ext = tokens + 2 * width
    frames, blocks = mesh.shape["frame"], mesh.shape["row"]
    slots = pairs * group
    n = max(pairs, 1)
    cfg = (heads, pairs, group, width, tokens, dim, frames, blocks)
    smem = pl.BlockSpec(memory_space=pltpu.SMEM)
    vmem = pl.BlockSpec(memory_space=pltpu.VMEM)
    dma = pltpu.SemaphoreType.DMA
    return pl.pallas_call(
        functools.partial(kernel, cfg),
        out_shape=[jax.ShapeDtypeStruct((tokens, packed), BF16)] * 3,
        in_specs=[smem, smem, smem, vmem, vmem, vmem, vmem],
        out_specs=[vmem, vmem, vmem],
        scratch_shapes=[
            pltpu.VMEM((heads, 2, tokens, dim), BF16),
            pltpu.VMEM((heads, 2, ext, dim), BF16),
            pltpu.VMEM((2, 2, width, packed), BF16),
            pltpu.VMEM((n, 3, group, 2, tokens, dim), BF16),
            pltpu.VMEM((ext, 3 * tokens), F32),
            pltpu.VMEM((max(slots, 1), ext, 3 * tokens), F32),
            pltpu.VMEM((max(slots, 1), ext, 3 * tokens), F32),
            pltpu.VMEM((n, 3, 4 * group, tokens), F32),
            pltpu.VMEM((n, 2, 4 * group, tokens), F32),
            pltpu.VMEM((n, 4 * group, tokens), F32),
            pltpu.VMEM((n, 2, 4 * group, tokens), F32),
            pltpu.VMEM((heads, tokens, dim), F32),
            pltpu.VMEM((n, 2, group, tokens, dim), BF16),
            pltpu.VMEM((n, 2, group, tokens, dim), BF16),
            pltpu.VMEM((heads, tokens, dim), F32),
            pltpu.VMEM((heads, tokens, dim), F32),
            pltpu.VMEM((2, heads, 2, width, dim), BF16),
            pltpu.VMEM((2, heads, 2, width, dim), BF16),
            dma((2, 2)),
            dma((2, 2)),
            dma((4, n, 2)),
            dma((4, n, 2)),
            dma((n + 1, 2)),
            dma((n + 1, 2)),
        ],
        compiler_params=pltpu.CompilerParams(
            collective_id=pairs, has_side_effects=True, vmem_limit_bytes=48 * 2**20
        ),
        cost_estimate=pl.CostEstimate(
            flops=12 * ext * tokens * dim * (heads + 2 * slots),
            bytes_accessed=14 * tokens * packed,
            transcendentals=ext * tokens * (heads + 2 * slots),
        ),
    )(info, penalty, offs, q, k, v, g)


def on_device(mesh, query_tok, key_tok, value_tok, grad_out, head_reach, tile_offset):
    _, rows_dev, width, packed = query_tok.shape
    heads = head_reach.shape[0]
    group = 2 if heads % 2 == 0 else 1
    flat = [x.reshape(rows_dev * width, packed) for x in (query_tok, key_tok, value_tok, grad_out)]
    reach = (head_reach == 1).astype(jnp.int32)
    ids = jnp.arange(heads, dtype=jnp.int32)
    before = jnp.sum(jnp.where(ids[None, :] < ids[:, None], reach[None, :], 0), axis=1)
    count = jnp.sum(reach)
    rank = jnp.where(reach == 1, before, count + ids - before)
    order = jnp.sum(jnp.where(rank[None, :] == ids[:, None], ids[None, :], 0), axis=1)
    info = jnp.stack([order, rank])
    penalty = jnp.where(ids < count, 0.0, MASKED).astype(F32)
    offs = tile_offset.astype(F32)
    all_pairs = heads // group
    sizes = SIZES(all_pairs)
    need = (count + group - 1) // group
    branch = sum((need > size).astype(jnp.int32) for size in sizes[:-1])
    run = [functools.partial(attention, mesh, size, group, width, heads) for size in sizes]
    if len(run) == 1:
        outs = run[0](info, penalty, offs, *flat)
    else:
        outs = lax.switch(branch, run, info, penalty, offs, *flat)
    return tuple(x.reshape(query_tok.shape) for x in outs)


def SIZES(all_pairs):
    return [all_pairs]


def solution(mesh):
    tok = P("frame", "row", None, None)
    return jax.shard_map(
        functools.partial(on_device, mesh),
        mesh=mesh,
        in_specs=(tok, tok, tok, tok, P(), P(None, "row")),
        out_specs=(tok, tok, tok),
        check_vma=False,
    )
```

time: 189 us -> 74.8 us (0.40); the launches traced: 186 us -> 73.8 us
  waiting for transfers between devices: 98.6 us -> 0 us
  Pallas kernels: 0 us -> 62.6 us
  starting transfers between devices: 25.2 us -> 0 us
  local copies, waits for them, and re-layouts: 31.2 us -> 7.6 us
  other arithmetic: 20.4 us -> 2.85 us
  matrix products: 9.2 us -> 0 us
    ppermute x8 -> x0, waiting for transfers between devices: 98.6 us -> none  [the longest x4 70.9 us: from_behind(): return lax.ppermute(block, axis, route)]
    pallas_call x0 -> x1, Pallas kernels: none -> 62.6 us  [attention(): pl.pallas_call(functools.partial(kernel, cfg), out_shape=[jax.ShapeDtypeS...]
    ppermute x8 -> x0, starting transfers between devices: 25.2 us -> none  [the longest x4 13.3 us: from_behind(): return lax.ppermute(block, axis, route)]
    dot_general x6 -> x0, matrix products: 9.2 us -> none  [the longest x1 2.33 us: tile_attend(): jnp.einsum('bmqk,bkmd->bqmd', dscores, key_w, preferred_element_type=jnp....]
    sub x1 -> x0, other arithmetic: 7.52 us -> none  [tile_attend(): expo = jnp.exp(scores - top)]
    slice x23 -> x0, local copies, waits for them, and re-layouts: 7 us -> none  [the longest x2 1.39 us: make_windows(): padded[:, 4:rows_dev + 4].reshape((frames + 2, tiles, 4, width) + trailing)]
    another operation x7 -> x0, local copies, waits for them, and re-layouts: 6.94 us -> none  [the longest x4 3.46 us: on_device(): jnp.stack([key_tok.reshape(1, rows_dev, width, heads, head_dim), value_to...]
    reshape x3 -> x0, local copies, waits for them, and re-layouts: 6.65 us -> none  [the longest x1 2.23 us: on_device(): query_grid = query_tok.reshape(tiles, 4 * width, heads, head_dim)]
  transfers between devices with their start and end apart: 8 -> 0, of which waited for: 5 -> 0; matrix products, arithmetic and copies ran while one was open for 8% -> 0% of each run, Pallas kernels for 0% -> 0%
where the time goes in v1:
time: 74.8 us; the launch traced here: 73.8 us
  Pallas kernels  62.6 us (84%)
  local copies, waits for them, and re-layouts  7.6 us (10%)
  other arithmetic  2.85 us (4%)
    pallas_call x1, Pallas kernels, attention(): pl.pallas_call(functools.partial(kernel, cfg), out_shape=[jax.ShapeDtypeS...  62.6 us
    unnamed x16, local copies, waits for them, and re-layouts  7.6 us

profile of v1, /device:TPU:11, one launch (start us, length us, event | category | flops | bytes accessed | tf_op | source)
XLA Modules:
  0.0 73.8 jit_solution(7924431795999970803)
XLA Ops:
  0.6 1.3 %fusion = s32[]{:T(128)} fusion(s32[20]{0:T(128)} %param.10), kind=kLoop, calls=%fused_computation.8 | loop fusion | flops 59 | bytes 84 | tf_op jit(solution)/shard_map/reduce_sum | solution.py:461
  1.9 0.0 copy-start.5
  1.9 0.7 compare_select_fusion.penalty
  2.6 0.0 copy-done.5
  2.6 0.1 select_reduce_fusion.1
  2.7 0.7 compare_select_fusion.1
  3.4 0.1 select_reduce_fusion
  3.5 0.0 copy-start.4
  3.5 0.7 copy-done.4
  4.2 0.1 copy.10
  4.3 0.0 copy-start
  4.3 1.1 %copy-done = bf16[1,8,16,2560]{3,2,1,0:T(8,128)(2,1)S(1)} copy-done((bf16[1,8,16,2560]{3,2,1,0:T(8,128)(2,1)S(1)}, bf16[1,8,16,2560]{3,2,1,0:T(8,128)(2,1)}, u32[]{:S(2)}) %copy-start) | copy-done | bytes 655384
  5.4 0.0 copy-start.1
  5.4 1.1 %copy-done.1 = bf16[1,8,16,2560]{3,2,1,0:T(8,128)(2,1)S(1)} copy-done((bf16[1,8,16,2560]{3,2,1,0:T(8,128)(2,1)S(1)}, bf16[1,8,16,2560]{3,2,1,0:T(8,128)(2,1)}, u32[]{:S(2)}) %copy-start.1) | copy-done | bytes 655384
  6.5 0.0 copy-start.2
  6.5 1.1 %copy-done.2 = bf16[1,8,16,2560]{3,2,1,0:T(8,128)(2,1)S(1)} copy-done((bf16[1,8,16,2560]{3,2,1,0:T(8,128)(2,1)S(1)}, bf16[1,8,16,2560]{3,2,1,0:T(8,128)(2,1)}, u32[]{:S(2)}) %copy-start.2) | copy-done | bytes 655384
  7.5 0.0 copy-start.3
  7.5 1.1 %copy-done.3 = bf16[1,8,16,2560]{3,2,1,0:T(8,128)(2,1)S(1)} copy-done((bf16[1,8,16,2560]{3,2,1,0:T(8,128)(2,1)S(1)}, bf16[1,8,16,2560]{3,2,1,0:T(8,128)(2,1)}, u32[]{:S(2)}) %copy-start.3) | copy-done | bytes 655384
  8.6 62.6 %shard_map.85 = (bf16[128,2560]{1,0:T(8,128)(2,1)S(1)}, bf16[128,2560]{1,0:T(8,128)(2,1)S(1)}, bf16[128,2560]{1,0:T(8,128)(2,1)S(1)}) custom-call(s32[2,20]{1,0:T(2,128)S(1)} %pad_add_fusion.info, f32[20]{0:T(128)S(1)} %compare_select_fusion.penalty, f32[8,2]{1,0:T(8,128)S(1)} %convert_element_type.7.offs, bf16[128,2560]{1,0:T(8,128)(2,1)S(1)} %bitcast.12, ...), custom_call_target="tpu_custom_call" | custom-call | flops 1887436800 | bytes 4587520 | tf_op jit(solution)/shard_map/pallas_call | solution.py:411
  71.3 0.8 %copy.14 = bf16[1,8,16,2560]{3,2,1,0:T(8,128)(2,1)} copy(bf16[1,8,16,2560]{3,2,1,0:T(8,128)(2,1)S(1)} %bitcast.11) | data formatting | bytes 1310720
  72.1 0.8 %copy.15 = bf16[1,8,16,2560]{3,2,1,0:T(8,128)(2,1)} copy(bf16[1,8,16,2560]{3,2,1,0:T(8,128)(2,1)S(1)} %bitcast.10) | data formatting | bytes 1310720
  72.9 0.8 %copy.16 = bf16[1,8,16,2560]{3,2,1,0:T(8,128)(2,1)} copy(bf16[1,8,16,2560]{3,2,1,0:T(8,128)(2,1)S(1)} %bitcast.9) | data formatting | bytes 1310720
  (3 shorter events, 0.0 us)
Async XLA Ops:
  1.9 0.7 copy-start.5
  3.5 0.7 copy-start.4
  4.3 1.1 %copy-start = (bf16[1,8,16,2560]{3,2,1,0:T(8,128)(2,1)S(1)}, bf16[1,8,16,2560]{3,2,1,0:T(8,128)(2,1)}, u32[]{:S(2)}) copy-start(bf16[1,8,16,2560]{3,2,1,0:T(8,128)(2,1)} %param.6) | copy-start | bytes 1966084
  5.4 1.1 %copy-start.1 = (bf16[1,8,16,2560]{3,2,1,0:T(8,128)(2,1)S(1)}, bf16[1,8,16,2560]{3,2,1,0:T(8,128)(2,1)}, u32[]{:S(2)}) copy-start(bf16[1,8,16,2560]{3,2,1,0:T(8,128)(2,1)} %param.7) | copy-start | bytes 1966084
  6.5 1.1 %copy-start.2 = (bf16[1,8,16,2560]{3,2,1,0:T(8,128)(2,1)S(1)}, bf16[1,8,16,2560]{3,2,1,0:T(8,128)(2,1)}, u32[]{:S(2)}) copy-start(bf16[1,8,16,2560]{3,2,1,0:T(8,128)(2,1)} %param.8) | copy-start | bytes 1966084
  7.5 1.1 %copy-start.3 = (bf16[1,8,16,2560]{3,2,1,0:T(8,128)(2,1)S(1)}, bf16[1,8,16,2560]{3,2,1,0:T(8,128)(2,1)}, u32[]{:S(2)}) copy-start(bf16[1,8,16,2560]{3,2,1,0:T(8,128)(2,1)} %param.9) | copy-start | bytes 1966084
